TPU v7x, 32 devices: a whole 2x2x4 slice. The times are simulated.
32 devices in a mesh: ctx: 8 (over z, x), tp: 4 (over y, core).
Axes of the slice: x: 2, y: 2, z: 4, core: 2. Of those that a mesh axis runs over, the one named last changes fastest.
Arguments:
- tokens: bfloat16 [4096, 3072], P(('ctx', 'tp')), may hold values from -6 to 6
- w_query: bfloat16 [3072, 4096], P(None, 'tp'), may hold values from -0.109375 to 0.109375
- w_key: bfloat16 [3072, 4096], P(None, 'tp'), may hold values from -0.109375 to 0.109375
- w_value: bfloat16 [3072, 4096], P(None, 'tp'), may hold values from -0.109375 to 0.109375
- norm_gain: float32 [4096], P('tp'), may hold values from 0.1 to 1.9
Outputs:
- attended: bfloat16 [4096, 4096], P('ctx', 'tp')
All inputs are finite; a program needn't handle non-finite values.
Results may differ from a plain program's by a relative error of at most 0.0062.
Values may be sent and summed in bfloat16 or wider, within the bound.
A program may use at most 64 MiB of HBM per device.

v0:
```python
import jax
import jax.numpy as jnp
from jax import lax
from jax.sharding import PartitionSpec as P

HEAD_DIM = 128
BLOCK = 512


EPSILON = 1e-06


def from_behind(value, axis, by):
    size = lax.axis_size(axis)
    pairs = [(i, i + by) for i in range(size) if 0 <= i + by < size]
    return lax.ppermute(value, axis, pairs)


def body(tokens, w_query, w_key, w_value, norm_gain):
    local_width = w_query.shape[1]
    head_count = local_width // HEAD_DIM
    piece_rows = lax.all_gather(tokens, "tp", axis=0, tiled=True)
    query_part = jnp.dot(piece_rows, w_query, preferred_element_type=jnp.float32).astype(
        jnp.bfloat16
    )
    key_part = jnp.dot(piece_rows, w_key, preferred_element_type=jnp.float32).astype(jnp.bfloat16)
    value_part = jnp.dot(piece_rows, w_value, preferred_element_type=jnp.float32).astype(
        jnp.bfloat16
    )
    projected = jnp.concatenate([query_part, key_part, value_part], axis=1)
    group_len = projected.shape[0]
    block_count = group_len // BLOCK
    shaped = projected.reshape(block_count, BLOCK, 3, head_count, HEAD_DIM)
    query_rows = shaped[:, :, 0]
    key_rows = shaped[:, :, 1]
    value_rows = shaped[:, :, 2]
    block_states = jnp.einsum(
        "bshd,bshe->bhde", key_rows, value_rows, preferred_element_type=jnp.float32
    )
    local_state = jnp.sum(block_states, axis=0)
    empty_state = jnp.zeros_like(local_state)

    def advance(step_index, carried):
        return from_behind(carried + local_state, "ctx", 1)

    prefix_state = lax.fori_loop(0, lax.axis_size("ctx") - 1, advance, empty_state)
    running = jnp.cumsum(block_states, axis=0)
    earlier = jnp.concatenate([jnp.zeros_like(block_states), running[:-1]], axis=0)
    block_start = prefix_state[None] + earlier
    scores = jnp.einsum("bqhd,bkhd->bhqk", query_rows, key_rows, preferred_element_type=jnp.float32)
    causal = jnp.arange(BLOCK)[:, None] >= jnp.arange(BLOCK)[None, :]
    scores = jnp.where(causal[None, None], scores, jnp.float32(0.0)).astype(jnp.bfloat16)
    inner = jnp.einsum("bhqk,bkhe->bqhe", scores, value_rows, preferred_element_type=jnp.float32)
    carried_part = jnp.einsum(
        "bqhd,bhde->bqhe",
        query_rows.astype(jnp.float32),
        block_start,
        precision=lax.Precision.HIGHEST,
    )
    mixed = inner + carried_part
    mean_square = jnp.mean(mixed * mixed, axis=-1, keepdims=True)
    normed = mixed * lax.rsqrt(mean_square + EPSILON) * norm_gain.reshape(head_count, HEAD_DIM)
    return normed.reshape(group_len, local_width).astype(jnp.bfloat16)


def solution(mesh):
    placed = (P(("ctx", "tp"), None), P(None, "tp"), P(None, "tp"), P(None, "tp"), P("tp"))
    return jax.shard_map(
        body, mesh=mesh, in_specs=placed, out_specs=P("ctx", "tp"), check_vma=False
    )
```

profile of v0, /device:TPU:26, one launch (start us, length us, event | category | flops | bytes accessed | tf_op | source)
XLA Modules:
  0.0 174.9 jit_solution(11872071652714777348)
XLA Ops:
  7.3 31.1 %all-gather.2.cloned.1.call-done = bf16[512,3072]{1,0:T(8,128)(2,1)} async-done(((bf16[128,3072]{1,0:T(8,128)(2,1)}), bf16[512,3072]{1,0:T(8,128)(2,1)}) %all-gather.2.cloned.1.call-update) | async-done | bytes 3145744 | tf_op jit(solution)/shard_map/all_gather | solution.py:22
  38.4 7.3 %convolution_convert_fusion = bf16[512,1024]{1,0:T(8,128)(2,1)S(1)} fusion(bf16[512,3072]{1,0:T(8,128)(2,1)} %all-gather.2.cloned.1.call-done, bf16[3072,1024]{1,0:T(8,128)(2,1)} %param.10), kind=kOutput, calls=%fused_computation.12 | convolution fusion | flops 3221749760 | bytes 10485760 | tf_op jit(solution)/shard_map/dot_general | solution.py:27
  45.8 6.4 %convolution_convert_fusion.1 = bf16[512,1024]{1,0:T(8,128)(2,1)S(1)} fusion(bf16[512,3072]{1,0:T(8,128)(2,1)S(1)} %copy-done.2, bf16[3072,1024]{1,0:T(8,128)(2,1)} %param.9), kind=kOutput, calls=%fused_computation.13 | convolution fusion | flops 3221749760 | bytes 10485760 | tf_op jit(solution)/shard_map/dot_general | solution.py:26
  52.2 3.4 %convolution_convert_fusion.2 = bf16[512,1024]{1,0:T(8,128)(2,1)S(1)} fusion(bf16[512,3072]{1,0:T(8,128)(2,1)S(1)} %copy-done.2, bf16[3072,1024]{1,0:T(8,128)(2,1)S(1)} %bitcast.44), kind=kOutput, calls=%fused_computation.14 | convolution fusion | flops 3221749760 | bytes 10485760 | tf_op jit(solution)/shard_map/dot_general | solution.py:23
  56.1 0.9 copy.14
  56.9 1.5 fusion.12
  60.3 5.1 %fusion = f32[8,128,512]{2,1,0:T(8,128)} fusion(pred[512,512]{1,0:T(8,128)(4,1)S(1)} %iota_compare_fusion, bf16[512,8,128]{0,2,1:T(8,128)(2,1)S(1)} %copy.10, bf16[1,512,1,8,128]{1,4,3,2,0:T(8,128)(2,1)S(1)} %copy.12, bf16[1,512,1,8,128]{4,3,2,1,0:T(8,128)(2,1)} %get-tuple-element.29), kind=kOutput, calls=%fused_computation.1 | convolution fusion | flops 1077936128 | bytes 5505024 | tf_op jit(solution)/shard_map/bhqk,bkhe->bqhe/dot_general | solution.py:53
  65.4 98.1 %while.10 = (s32[]{:T(128)}, f32[8,128,128]{2,1,0:T(8,128)S(1)}, f32[8,128,128]{2,1,0:T(8,128)S(1)}, s32[]{:T(128)}) while((s32[]{:T(128)}, f32[8,128,128]{2,1,0:T(8,128)S(1)}, f32[8,128,128]{2,1,0:T(8,128)S(1)}, s32[]{:T(128)}) %tuple.21), condition=%wide.region_1.0_spmd, body=%wide.region_0.0_spmd.sunk | while | flops 131074 | bytes 3670109 | solution.py:46
  65.5 1.4 collective-permute-start
  66.9 14.7 %collective-permute-done = f32[8,128,128]{2,1,0:T(8,128)S(1)} collective-permute-done((f32[8,128,128]{2,1,0:T(8,128)S(1)}, f32[8,128,128]{2,1,0:T(8,128)S(1)}, u32[]{:S(2)}, u32[]{:S(2)}) %collective-permute-start) | collective-permute-done | bytes 524320 | tf_op jit(solution)/shard_map/while/body/eval_jaxpr/ppermute | solution.py:16
  81.6 1.3 collective-permute-start
  82.9 13.8 %collective-permute-done = f32[8,128,128]{2,1,0:T(8,128)S(1)} collective-permute-done((f32[8,128,128]{2,1,0:T(8,128)S(1)}, f32[8,128,128]{2,1,0:T(8,128)S(1)}, u32[]{:S(2)}, u32[]{:S(2)}) %collective-permute-start) | collective-permute-done | bytes 524320 | tf_op jit(solution)/shard_map/while/body/eval_jaxpr/ppermute | solution.py:16
  96.9 1.3 collective-permute-start
  98.2 13.6 %collective-permute-done = f32[8,128,128]{2,1,0:T(8,128)S(1)} collective-permute-done((f32[8,128,128]{2,1,0:T(8,128)S(1)}, f32[8,128,128]{2,1,0:T(8,128)S(1)}, u32[]{:S(2)}, u32[]{:S(2)}) %collective-permute-start) | collective-permute-done | bytes 524320 | tf_op jit(solution)/shard_map/while/body/eval_jaxpr/ppermute | solution.py:16
  111.8 1.3 collective-permute-start
  113.1 12.9 %collective-permute-done = f32[8,128,128]{2,1,0:T(8,128)S(1)} collective-permute-done((f32[8,128,128]{2,1,0:T(8,128)S(1)}, f32[8,128,128]{2,1,0:T(8,128)S(1)}, u32[]{:S(2)}, u32[]{:S(2)}) %collective-permute-start) | collective-permute-done | bytes 524320 | tf_op jit(solution)/shard_map/while/body/eval_jaxpr/ppermute | solution.py:16
  126.1 1.3 collective-permute-start
  127.4 12.0 %collective-permute-done = f32[8,128,128]{2,1,0:T(8,128)S(1)} collective-permute-done((f32[8,128,128]{2,1,0:T(8,128)S(1)}, f32[8,128,128]{2,1,0:T(8,128)S(1)}, u32[]{:S(2)}, u32[]{:S(2)}) %collective-permute-start) | collective-permute-done | bytes 524320 | tf_op jit(solution)/shard_map/while/body/eval_jaxpr/ppermute | solution.py:16
  139.4 1.3 collective-permute-start
  140.7 11.1 %collective-permute-done = f32[8,128,128]{2,1,0:T(8,128)S(1)} collective-permute-done((f32[8,128,128]{2,1,0:T(8,128)S(1)}, f32[8,128,128]{2,1,0:T(8,128)S(1)}, u32[]{:S(2)}, u32[]{:S(2)}) %collective-permute-start) | collective-permute-done | bytes 524320 | tf_op jit(solution)/shard_map/while/body/eval_jaxpr/ppermute | solution.py:16
  151.8 1.3 collective-permute-start
  153.1 10.4 %collective-permute-done = f32[8,128,128]{2,1,0:T(8,128)S(1)} collective-permute-done((f32[8,128,128]{2,1,0:T(8,128)S(1)}, f32[8,128,128]{2,1,0:T(8,128)S(1)}, u32[]{:S(2)}, u32[]{:S(2)}) %collective-permute-start) | collective-permute-done | bytes 524320 | tf_op jit(solution)/shard_map/while/body/eval_jaxpr/ppermute | solution.py:16
  163.5 2.8 %fusion.5 = (f32[512,8]{0,1:T(8,128)S(1)}, f32[8,128,512]{2,1,0:T(8,128)S(1)}) fusion(f32[8,128,512]{2,1,0:T(8,128)} %fusion, f32[8,128,128]{2,1,0:T(8,128)S(1)} %get-tuple-element.22, bf16[1,512,1,8,128]{4,3,2,1,0:T(8,128)(2,1)S(1)} %copy-done), kind=kOutput, calls=%fused_computation.8 | convolution fusion | flops 806875136 | bytes 5783552 | tf_op jit(solution)/shard_map/bqhd,bhde->bqhe/dot_general | solution.py:54
  166.7 1.3 copy.9
  (28 shorter events, 3.8 us)
Async XLA Ops:
  6.5 31.9 %all-gather.2.cloned.1.call-start = ((), (), s32[]{:S(2)}) async-start(), calls=%async_computation | async-start | bytes 3932160 | tf_op jit(solution)/shard_map/all_gather | solution.py:22
  38.4 7.3 %copy-start.2 = (bf16[512,3072]{1,0:T(8,128)(2,1)S(1)}, bf16[512,3072]{1,0:T(8,128)(2,1)}, u32[]{:S(2)}) copy-start(bf16[512,3072]{1,0:T(8,128)(2,1)} %all-gather.2.cloned.1.call-done) | copy-start | bytes 9437188
  38.4 13.7 %slice-start = ((s8[6291456]{0:T(1024)(128)(4,1)}), s8[4194304]{0:T(1024)(128)(4,1)S(1)}, s32[]{:S(2)}) async-start(s8[6291456]{0:T(1024)(128)(4,1)} %bitcast.43), calls=%async_computation.1 | async-start | bytes 8388608
  45.7 6.4 %slice-start.1 = ((s8[6291456]{0:T(1024)(128)(4,1)}), s8[2097152]{0:T(1024)(128)(4,1)S(1)}, s32[]{:S(2)}) async-start(s8[6291456]{0:T(1024)(128)(4,1)} %bitcast.43), calls=%async_computation.2 | async-start | bytes 4194304
  65.4 98.1 %copy-start = (bf16[1,512,1,8,128]{4,3,2,1,0:T(8,128)(2,1)S(1)}, bf16[1,512,1,8,128]{4,3,2,1,0:T(8,128)(2,1)}, u32[]{:S(2)}) copy-start(bf16[1,512,1,8,128]{4,3,2,1,0:T(8,128)(2,1)} %get-tuple-element.29) | copy-start | bytes 3145732
  65.5 16.1 %collective-permute-start = (f32[8,128,128]{2,1,0:T(8,128)S(1)}, f32[8,128,128]{2,1,0:T(8,128)S(1)}, u32[]{:S(2)}, u32[]{:S(2)}) collective-permute-start(f32[8,128,128]{2,1,0:T(8,128)S(1)} %add.37), channel_id=1, source_target_pairs={{0,4},{4,8},{8,12},{12,16},{16,20},{20,24},{24,28},{1,5},{5,9},{9,... | collective-permute-start | bytes 1572872 | tf_op jit(solution)/shard_map/while/body/eval_jaxpr/ppermute | solution.py:16
  81.6 15.1 %collective-permute-start = (f32[8,128,128]{2,1,0:T(8,128)S(1)}, f32[8,128,128]{2,1,0:T(8,128)S(1)}, u32[]{:S(2)}, u32[]{:S(2)}) collective-permute-start(f32[8,128,128]{2,1,0:T(8,128)S(1)} %add.37), channel_id=1, source_target_pairs={{0,4},{4,8},{8,12},{12,16},{16,20},{20,24},{24,28},{1,5},{5,9},{9,... | collective-permute-start | bytes 1572872 | tf_op jit(solution)/shard_map/while/body/eval_jaxpr/ppermute | solution.py:16
  96.9 14.9 %collective-permute-start = (f32[8,128,128]{2,1,0:T(8,128)S(1)}, f32[8,128,128]{2,1,0:T(8,128)S(1)}, u32[]{:S(2)}, u32[]{:S(2)}) collective-permute-start(f32[8,128,128]{2,1,0:T(8,128)S(1)} %add.37), channel_id=1, source_target_pairs={{0,4},{4,8},{8,12},{12,16},{16,20},{20,24},{24,28},{1,5},{5,9},{9,... | collective-permute-start | bytes 1572872 | tf_op jit(solution)/shard_map/while/body/eval_jaxpr/ppermute | solution.py:16
  111.8 14.2 %collective-permute-start = (f32[8,128,128]{2,1,0:T(8,128)S(1)}, f32[8,128,128]{2,1,0:T(8,128)S(1)}, u32[]{:S(2)}, u32[]{:S(2)}) collective-permute-start(f32[8,128,128]{2,1,0:T(8,128)S(1)} %add.37), channel_id=1, source_target_pairs={{0,4},{4,8},{8,12},{12,16},{16,20},{20,24},{24,28},{1,5},{5,9},{9,... | collective-permute-start | bytes 1572872 | tf_op jit(solution)/shard_map/while/body/eval_jaxpr/ppermute | solution.py:16
  126.1 13.3 %collective-permute-start = (f32[8,128,128]{2,1,0:T(8,128)S(1)}, f32[8,128,128]{2,1,0:T(8,128)S(1)}, u32[]{:S(2)}, u32[]{:S(2)}) collective-permute-start(f32[8,128,128]{2,1,0:T(8,128)S(1)} %add.37), channel_id=1, source_target_pairs={{0,4},{4,8},{8,12},{12,16},{16,20},{20,24},{24,28},{1,5},{5,9},{9,... | collective-permute-start | bytes 1572872 | tf_op jit(solution)/shard_map/while/body/eval_jaxpr/ppermute | solution.py:16
  139.4 12.4 %collective-permute-start = (f32[8,128,128]{2,1,0:T(8,128)S(1)}, f32[8,128,128]{2,1,0:T(8,128)S(1)}, u32[]{:S(2)}, u32[]{:S(2)}) collective-permute-start(f32[8,128,128]{2,1,0:T(8,128)S(1)} %add.37), channel_id=1, source_target_pairs={{0,4},{4,8},{8,12},{12,16},{16,20},{20,24},{24,28},{1,5},{5,9},{9,... | collective-permute-start | bytes 1572872 | tf_op jit(solution)/shard_map/while/body/eval_jaxpr/ppermute | solution.py:16
  151.8 11.7 %collective-permute-start = (f32[8,128,128]{2,1,0:T(8,128)S(1)}, f32[8,128,128]{2,1,0:T(8,128)S(1)}, u32[]{:S(2)}, u32[]{:S(2)}) collective-permute-start(f32[8,128,128]{2,1,0:T(8,128)S(1)} %add.37), channel_id=1, source_target_pairs={{0,4},{4,8},{8,12},{12,16},{16,20},{20,24},{24,28},{1,5},{5,9},{9,... | collective-permute-start | bytes 1572872 | tf_op jit(solution)/shard_map/while/body/eval_jaxpr/ppermute | solution.py:16
  163.5 2.8 %copy-start.1 = (f32[1024]{0:T(1024)S(1)}, f32[1024]{0:T(1024)}, u32[]{:S(2)}) copy-start(f32[1024]{0:T(1024)} %param.11) | copy-start | bytes 12292
Sparse Core Ops, SparseCore 0:
  8.9 29.4 all-gather.1
where the time goes:
time: 178 us; the launch traced here: 175 us
  waiting for transfers between devices  120 us (67%)
  matrix products  25.4 us (14%)
  between operations  13.5 us (8%)
  starting transfers between devices  9.18 us (5%)
  local copies, waits for them, and re-layouts  5.09 us (3%)
    ppermute x7, waiting for transfers between devices, from_behind(): return lax.ppermute(value, axis, pairs)  88.4 us
    all_gather x1, waiting for transfers between devices, body(): piece_rows = lax.all_gather(tokens, 'tp', axis=0, tiled=True)  31.1 us
    ppermute x7, starting transfers between devices, from_behind(): return lax.ppermute(value, axis, pairs)  9.18 us
    dot_general x1, matrix products, body(): jnp.dot(piece_rows, w_value, preferred_element_type=jnp.float32)  7.29 us
    dot_general x1, matrix products, body(): jnp.dot(piece_rows, w_key, preferred_element_type=jnp.float32)  6.39 us
    dot_general x1, matrix products, body(): jnp.einsum('bhqk,bkhe->bqhe', scores, value_rows, preferred_element_type=...  5.11 us
  transfers between devices with their start and end apart: 8, of which 8 were waited for; matrix products, arithmetic and copies ran while one was open for 0% of the time, Pallas kernels for 0%

commit v1 on v0

v1 whole, which is shorter than its diff:
```python
import functools

import jax
import jax.numpy as jnp
from jax import lax
from jax.experimental import pallas as pl
from jax.experimental.pallas import tpu as pltpu
from jax.sharding import PartitionSpec as P

HEAD_DIM = 128
BLOCK = 512
EPSILON = 1e-06
MESH = pl.DeviceIdType.MESH
TILE_N = 256
CHUNKS = 6
F32 = jnp.float32
BF16 = jnp.bfloat16


def kernel(
    nctx, ntp, tok, wq, wk, wv, gain, out,
    xbuf, wbuf, acc, kvq, mixed, st, s1, r1, pin, pout, pown, s2, r2,
    wsem, osem, ysend, yrecv, ssend, srecv, fsend, frecv,
    s1send, s1recv, csend, crecv, s2send, s2recv,
):
    ctx, tp = lax.axis_index("ctx"), lax.axis_index("tp")
    rows, depth = tok.shape
    width = wq.shape[1]
    tiles = width // TILE_N
    heads = width // HEAD_DIM
    half = heads // 2
    chips, pairs = ntp // 2, nctx // 2
    core, chip = tp % 2, tp // 2
    sib = tp + 1 - 2 * core
    odd, pair = ctx % 2, ctx // 2
    partner = ctx + 1 - 2 * odd
    ck = depth // CHUNKS
    duo = 2 * rows

    def at_rows(index, count):
        return pl.ds(pl.multiple_of(index * count, count), count)

    weights = (wk, wv, wq)

    def weight_copy(m, n):
        cols = pl.ds(pl.multiple_of(n * TILE_N, TILE_N), TILE_N)
        return pltpu.make_async_copy(
            weights[m].at[:, cols], wbuf.at[m, :, cols], wsem.at[m * tiles + n]
        )

    own = pltpu.make_async_copy(tok, xbuf.at[at_rows(tp, rows), :], osem)
    own.start()
    for m in range(3):
        for n in range(tiles):
            weight_copy(m, n).start()

    barrier = pltpu.get_barrier_semaphore()

    def greet(c, t):
        pl.semaphore_signal(barrier, inc=1, device_id={"ctx": c, "tp": t}, device_id_type=MESH)

    greet(ctx, sib)
    for j in range(1, chips):
        greet(ctx, ((chip + j) % chips) * 2 + core)
    greet(partner, tp)

    @pl.when(pair > 0)
    def _():
        greet(ctx - 2, tp)

    @pl.when(pair < pairs - 1)
    def _():
        greet(ctx + 2, tp)

    inner = jnp.minimum(pair, 1) + jnp.minimum(pairs - 1 - pair, 1)
    pl.semaphore_wait(barrier, chips + 1 + inner)

    def cols_of(c):
        return pl.ds(c * ck, ck)

    def y_copy(j, c, source):
        return pltpu.make_async_remote_copy(
            src_ref=tok.at[:, cols_of(c)],
            dst_ref=xbuf.at[at_rows(source, rows), cols_of(c)],
            send_sem=ysend.at[j - 1, c],
            recv_sem=yrecv.at[j - 1, c],
            device_id={"ctx": ctx, "tp": ((chip + j) % chips) * 2 + core},
            device_id_type=MESH,
        )

    def sib_copy(source):
        return pltpu.make_async_remote_copy(
            src_ref=tok,
            dst_ref=xbuf.at[at_rows(source, rows), :],
            send_sem=ssend,
            recv_sem=srecv,
            device_id={"ctx": ctx, "tp": sib},
            device_id_type=MESH,
        )

    def pass_on(j, c, source):
        place = xbuf.at[at_rows(source, rows), cols_of(c)]
        return pltpu.make_async_remote_copy(
            src_ref=place,
            dst_ref=place,
            send_sem=fsend.at[j - 1, c],
            recv_sem=frecv.at[j - 1, c],
            device_id={"ctx": ctx, "tp": sib},
            device_id_type=MESH,
        )

    sib_copy(tp).start()
    for c in range(CHUNKS):
        for j in range(1, chips):
            y_copy(j, c, tp).start()

    own.wait()
    sib_copy(sib).wait_recv()
    mine = at_rows(chip, duo)
    for m in range(3):

        @pl.loop(0, tiles)
        def _(n, m=m):
            weight_copy(m, n).wait()
            cols = pl.ds(pl.multiple_of(n * TILE_N, TILE_N), TILE_N)
            done = jnp.dot(xbuf[mine, :], wbuf[m, :, cols], preferred_element_type=F32)
            kvq[m, mine, cols] = done.astype(BF16)

    def origin(j):
        return (chip - j + chips) % chips

    def wave(c, low, high):
        for j in range(1, chips):
            there = at_rows(origin(j), duo)

            @pl.loop(low * tiles, high * tiles)
            def _(index):
                m, n = index // tiles, index % tiles
                cols = pl.ds(pl.multiple_of(n * TILE_N, TILE_N), TILE_N)
                term = jnp.dot(
                    xbuf[there, cols_of(c)],
                    wbuf[m, cols_of(c), cols],
                    preferred_element_type=F32,
                )
                if c > 0:
                    term += acc[m, there, cols]
                if c < CHUNKS - 1:
                    acc[m, there, cols] = term
                else:
                    kvq[m, there, cols] = term.astype(BF16)

    for c in range(CHUNKS):
        for j in range(1, chips):
            source = origin(j) * 2 + core
            y_copy(j, c, source).wait_recv()
            pass_on(j, c, source).start()
        for j in range(1, chips):
            pass_on(j, c, origin(j) * 2 + 1 - core).wait_recv()
        if c < CHUNKS - 1:
            wave(c, 0, 3)
        else:
            wave(c, 0, 2)

    def head_cols(h):
        return pl.ds(pl.multiple_of(h * HEAD_DIM, HEAD_DIM), HEAD_DIM)

    def outer(h):
        return lax.dot_general(
            kvq[0, :, head_cols(h)], kvq[1, :, head_cols(h)],
            (((0,), (0,)), ((), ())), preferred_element_type=F32,
        )

    def to_partner(buffer, landing, send, recv, i):
        return pltpu.make_async_remote_copy(
            src_ref=buffer.at[i],
            dst_ref=landing.at[i],
            send_sem=send.at[i],
            recv_sem=recv.at[i],
            device_id={"ctx": partner, "tp": tp},
            device_id_type=MESH,
        )

    def first(i):
        return to_partner(s1, r1, s1send, s1recv, i)

    def second(i):
        return to_partner(s2, r2, s2send, s2recv, i)

    def onward(i):
        return pltpu.make_async_remote_copy(
            src_ref=pout.at[i],
            dst_ref=pin.at[i],
            send_sem=csend.at[i],
            recv_sem=crecv.at[i],
            device_id={"ctx": jnp.minimum(ctx + 2, nctx - 2 + odd), "tp": tp},
            device_id_type=MESH,
        )

    @pl.loop(0, half)
    def _(i):
        s1[i] = outer((1 - odd) * half + i).astype(BF16)
        first(i).start()

    @pl.loop(0, half)
    def _(i):
        st[i] = outer(odd * half + i)

    wave(CHUNKS - 1, 2, 3)

    mid = BLOCK // 2

    def intra(h):
        cols = head_cols(h)
        causal = lax.broadcasted_iota(jnp.int32, (mid, mid), 0) >= lax.broadcasted_iota(
            jnp.int32, (mid, mid), 1
        )
        top, low = pl.ds(0, mid), pl.ds(mid, mid)

        def score(a, b):
            return lax.dot_general(
                kvq[2, a, cols], kvq[0, b, cols],
                (((1,), (1,)), ((), ())), preferred_element_type=F32,
            )

        s00 = jnp.where(causal, score(top, top), 0.0).astype(BF16)
        s10 = score(low, top).astype(BF16)
        s11 = jnp.where(causal, score(low, low), 0.0).astype(BF16)
        v0, v1 = kvq[1, top, cols], kvq[1, low, cols]
        mixed[h, top, :] = jnp.dot(s00, v0, preferred_element_type=F32)
        mixed[h, low, :] = jnp.dot(s10, v0, preferred_element_type=F32) + jnp.dot(
            s11, v1, preferred_element_type=F32
        )

    def finish(h, state):
        cols = head_cols(h)
        full = mixed[h] + jnp.dot(kvq[2, :, cols], state, preferred_element_type=F32)
        mean_square = jnp.mean(full * full, axis=-1, keepdims=True)
        out[:, cols] = (full * lax.rsqrt(mean_square + EPSILON) * gain[pl.ds(h, 1), :]).astype(BF16)

    @pl.when(pair == 0)
    def _():
        pin[...] = jnp.zeros_like(pin)

    ahead = jnp.minimum(2 * pair, heads)

    @pl.loop(0, ahead)
    def _(h):
        intra(h)

    @pl.loop(0, half)
    def _(i):
        first(i).wait_recv()

        @pl.when(pair > 0)
        def _():
            onward(i).wait_recv()

        before = pin[i].astype(F32)
        here, beside = st[i], r1[i].astype(F32)

        @pl.when(pair < pairs - 1)
        def _():
            pout[i] = (before + here + beside).astype(BF16)
            onward(i).start()

        s2[i] = (before + jnp.where(odd == 0, here, 0.0)).astype(BF16)
        second(i).start()
        pown[i] = (before + jnp.where(odd == 1, beside, 0.0)).astype(BF16)

        @pl.loop(jnp.minimum(ahead + 2 * i, heads), jnp.minimum(ahead + 2 * i + 2, heads))
        def _(h):
            intra(h)

    @pl.loop(0, half)
    def _(i):
        finish(odd * half + i, pown[i])

    @pl.loop(0, half)
    def _(i):
        second(i).wait_recv()
        finish((1 - odd) * half + i, r2[i])

    sib_copy(tp).wait_send()
    for c in range(CHUNKS):
        for j in range(1, chips):
            y_copy(j, c, tp).wait_send()
            pass_on(j, c, origin(j) * 2 + core).wait_send()

    @pl.loop(0, half)
    def _(i):
        first(i).wait_send()
        second(i).wait_send()

        @pl.when(pair < pairs - 1)
        def _():
            onward(i).wait_send()


def body(nctx, ntp, tokens, w_query, w_key, w_value, norm_gain):
    rows, depth = tokens.shape
    width = w_query.shape[1]
    heads = width // HEAD_DIM
    half, chips = heads // 2, ntp // 2
    tiles = width // TILE_N
    assert rows * ntp == BLOCK
    anywhere = pl.BlockSpec(memory_space=pl.ANY)
    vmem = pl.BlockSpec(memory_space=pltpu.VMEM)
    dma = pltpu.SemaphoreType.DMA
    small = pltpu.VMEM((half, HEAD_DIM, HEAD_DIM), BF16)
    hops = (max(chips - 1, 1), CHUNKS)
    return pl.pallas_call(
        functools.partial(kernel, nctx, ntp),
        out_shape=jax.ShapeDtypeStruct((BLOCK, width), BF16),
        in_specs=[anywhere] * 4 + [vmem],
        out_specs=vmem,
        scratch_shapes=[
            pltpu.VMEM((BLOCK, depth), BF16),
            pltpu.VMEM((3, depth, width), BF16),
            pltpu.VMEM((3, BLOCK, width), F32),
            pltpu.VMEM((3, BLOCK, width), BF16),
            pltpu.VMEM((heads, BLOCK, HEAD_DIM), F32),
            pltpu.VMEM((half, HEAD_DIM, HEAD_DIM), F32),
            small, small, small, small, small, small, small,
            dma((3 * tiles,)), dma, dma(hops), dma(hops), dma, dma, dma(hops), dma(hops),
            dma((half,)), dma((half,)), dma((half,)), dma((half,)), dma((half,)), dma((half,)),
        ],
        compiler_params=pltpu.CompilerParams(
            collective_id=0, has_side_effects=True, vmem_limit_bytes=60 * 2**20
        ),
        cost_estimate=pl.CostEstimate(
            flops=2 * BLOCK * depth * 3 * width, bytes_accessed=6 * depth * width, transcendentals=0
        ),
    )(tokens, w_query, w_key, w_value, norm_gain.reshape(heads, HEAD_DIM))


def solution(mesh):
    placed = (P(("ctx", "tp"), None), P(None, "tp"), P(None, "tp"), P(None, "tp"), P("tp"))
    return jax.shard_map(
        functools.partial(body, mesh.shape["ctx"], mesh.shape["tp"]),
        mesh=mesh, in_specs=placed, out_specs=P("ctx", "tp"), check_vma=False,
    )
```

time: 178 us -> 58.8 us (0.33); the launches traced: 175 us -> 58.3 us
  waiting for transfers between devices: 120 us -> 0 us
  Pallas kernels: 0 us -> 56.1 us
  matrix products: 25.4 us -> 0 us
  between operations: 13.5 us -> 0.01 us
  starting transfers between devices: 9.18 us -> 0 us
  local copies, waits for them, and re-layouts: 5.09 us -> 2.26 us
    ppermute x7 -> x0, waiting for transfers between devices: 88.4 us -> none  [from_behind(): return lax.ppermute(value, axis, pairs)]
    pallas_call x0 -> x1, Pallas kernels: none -> 56.1 us  [body(): pl.pallas_call(functools.partial(kernel, nctx, ntp), out_shape=jax.ShapeD...]
    all_gather x1 -> x0, waiting for transfers between devices: 31.1 us -> none  [body(): piece_rows = lax.all_gather(tokens, 'tp', axis=0, tiled=True)]
    dot_general x6 -> x0, matrix products: 25.4 us -> none  [the longest x1 7.29 us: body(): jnp.dot(piece_rows, w_value, preferred_element_type=jnp.float32)]
    ppermute x7 -> x0, starting transfers between devices: 9.18 us -> none  [from_behind(): return lax.ppermute(value, axis, pairs)]
  transfers between devices with their start and end apart: 8 -> 0, of which waited for: 8 -> 0; matrix products, arithmetic and copies ran while one was open for 0% -> 0% of each run, Pallas kernels for 0% -> 0%
where the time goes in v1:
time: 58.8 us; the launch traced here: 58.3 us
  Pallas kernels  56.1 us (95%)
  local copies, waits for them, and re-layouts  2.26 us (4%)
    pallas_call x1, Pallas kernels, body(): pl.pallas_call(functools.partial(kernel, nctx, ntp), out_shape=jax.ShapeD...  56.1 us
    unnamed x1, local copies, waits for them, and re-layouts  2.26 us

profile of v1, /device:TPU:26, one launch (start us, length us, event | category | flops | bytes accessed | tf_op | source)
XLA Modules:
  0.0 58.3 jit_solution(1329521437925021124)
XLA Ops:
  0.0 56.1 %shard_map.55 = bf16[512,1024]{1,0:T(8,128)(2,1)} custom-call(bf16[128,3072]{1,0:T(8,128)(2,1)} %tok.1, bf16[3072,1024]{1,0:T(8,128)(2,1)} %wq.1, bf16[3072,1024]{1,0:T(8,128)(2,1)} %wk.1, bf16[3072,1024]{1,0:T(8,128)(2,1)} %wv.1, f32[8,128]{1,0:T(8,128)} %bitcast.1), custom_call_target="tpu_custom_call" | custom-call | flops 9663676416 | bytes 18874368 | tf_op jit(solution)/shard_map/pallas_call | solution.py:311
  56.1 2.3 %copy.7 = bf16[512,1024]{1,0:T(8,128)(2,1)} copy(bf16[512,1024]{1,0:T(8,128)(2,1)} %shard_map.55) | data formatting | bytes 2097152

commit v2 on v1

--- a/solution.py
+++ b/solution.py
@@ -11,8 +11,9 @@
 BLOCK = 512
 EPSILON = 1e-06
 MESH = pl.DeviceIdType.MESH
-TILE_N = 256
-CHUNKS = 6
+TILE_N = 512
+TWELFTHS = (0, 4, 8, 10, 11, 12)
+CHUNKS = len(TWELFTHS) - 1
 F32 = jnp.float32
 BF16 = jnp.bfloat16
 
@@ -34,7 +35,7 @@
     sib = tp + 1 - 2 * core
     odd, pair = ctx % 2, ctx // 2
     partner = ctx + 1 - 2 * odd
-    ck = depth // CHUNKS
+    cuts = [depth * part // 12 for part in TWELFTHS]
     duo = 2 * rows
 
     def at_rows(index, count):
@@ -76,7 +77,7 @@
     pl.semaphore_wait(barrier, chips + 1 + inner)
 
     def cols_of(c):
-        return pl.ds(c * ck, ck)
+        return pl.ds(cuts[c], cuts[c + 1] - cuts[c])
 
     def y_copy(j, c, source):
         return pltpu.make_async_remote_copy(
@@ -126,6 +127,25 @@
             done = jnp.dot(xbuf[mine, :], wbuf[m, :, cols], preferred_element_type=F32)
             kvq[m, mine, cols] = done.astype(BF16)
 
+    def head_cols(h):
+        return pl.ds(pl.multiple_of(h * HEAD_DIM, HEAD_DIM), HEAD_DIM)
+
+    def outer(h, where):
+        return lax.dot_general(
+            kvq[0, where, head_cols(h)], kvq[1, where, head_cols(h)],
+            (((0,), (0,)), ((), ())), preferred_element_type=F32,
+        )
+
+    def whole_outer(h):
+        total = st[h]
+        for j in range(1, chips):
+            total += outer(h, at_rows(origin(j), duo))
+        return total
+
+    @pl.loop(0, heads)
+    def _(h):
+        st[h] = outer(h, mine)
+
     def origin(j):
         return (chip - j + chips) % chips
 
@@ -133,21 +153,17 @@
         for j in range(1, chips):
             there = at_rows(origin(j), duo)
 
-            @pl.loop(low * tiles, high * tiles)
-            def _(index):
-                m, n = index // tiles, index % tiles
-                cols = pl.ds(pl.multiple_of(n * TILE_N, TILE_N), TILE_N)
+            @pl.loop(low, high)
+            def _(m):
                 term = jnp.dot(
-                    xbuf[there, cols_of(c)],
-                    wbuf[m, cols_of(c), cols],
-                    preferred_element_type=F32,
+                    xbuf[there, cols_of(c)], wbuf[m, cols_of(c), :], preferred_element_type=F32
                 )
                 if c > 0:
-                    term += acc[m, there, cols]
+                    term += acc[m, there, :]
                 if c < CHUNKS - 1:
-                    acc[m, there, cols] = term
+                    acc[m, there, :] = term
                 else:
-                    kvq[m, there, cols] = term.astype(BF16)
+                    kvq[m, there, :] = term.astype(BF16)
 
     for c in range(CHUNKS):
         for j in range(1, chips):
@@ -161,15 +177,6 @@
         else:
             wave(c, 0, 2)
 
-    def head_cols(h):
-        return pl.ds(pl.multiple_of(h * HEAD_DIM, HEAD_DIM), HEAD_DIM)
-
-    def outer(h):
-        return lax.dot_general(
-            kvq[0, :, head_cols(h)], kvq[1, :, head_cols(h)],
-            (((0,), (0,)), ((), ())), preferred_element_type=F32,
-        )
-
     def to_partner(buffer, landing, send, recv, i):
         return pltpu.make_async_remote_copy(
             src_ref=buffer.at[i],
@@ -198,12 +205,13 @@
 
     @pl.loop(0, half)
     def _(i):
-        s1[i] = outer((1 - odd) * half + i).astype(BF16)
+        s1[i] = whole_outer((1 - odd) * half + i).astype(BF16)
         first(i).start()
 
     @pl.loop(0, half)
     def _(i):
-        st[i] = outer(odd * half + i)
+        h = odd * half + i
+        st[h] = whole_outer(h)
 
     wave(CHUNKS - 1, 2, 3)
 
@@ -256,7 +264,7 @@
             onward(i).wait_recv()
 
         before = pin[i].astype(F32)
-        here, beside = st[i], r1[i].astype(F32)
+        here, beside = st[odd * half + i], r1[i].astype(F32)
 
         @pl.when(pair < pairs - 1)
         def _():
@@ -319,7 +327,7 @@
             pltpu.VMEM((3, BLOCK, width), F32),
             pltpu.VMEM((3, BLOCK, width), BF16),
             pltpu.VMEM((heads, BLOCK, HEAD_DIM), F32),
-            pltpu.VMEM((half, HEAD_DIM, HEAD_DIM), F32),
+            pltpu.VMEM((heads, HEAD_DIM, HEAD_DIM), F32),
             small, small, small, small, small, small, small,
             dma((3 * tiles,)), dma, dma(hops), dma(hops), dma, dma, dma(hops), dma(hops),
             dma((half,)), dma((half,)), dma((half,)), dma((half,)), dma((half,)), dma((half,)),

time: 58.8 us -> 46.8 us (0.80)
  Pallas kernels: 56.1 us -> 44.4 us
    pallas_call x1, Pallas kernels: 56.1 us -> 44.4 us  [body(): pl.pallas_call(functools.partial(kernel, nctx, ntp), out_shape=jax.ShapeD...]
where the time goes in v2:
time: 46.8 us; the launch traced here: 46.7 us
  Pallas kernels  44.4 us (95%)
  local copies, waits for them, and re-layouts  2.26 us (5%)
    pallas_call x1, Pallas kernels, body(): pl.pallas_call(functools.partial(kernel, nctx, ntp), out_shape=jax.ShapeD...  44.4 us
    unnamed x1, local copies, waits for them, and re-layouts  2.26 us

profile of v2, /device:TPU:26, one launch (start us, length us, event | category | flops | bytes accessed | tf_op | source)
XLA Modules:
  0.0 46.7 jit_solution(6353532459612667486)
XLA Ops:
  0.0 44.4 %shard_map.55 = bf16[512,1024]{1,0:T(8,128)(2,1)} custom-call(bf16[128,3072]{1,0:T(8,128)(2,1)} %tok.1, bf16[3072,1024]{1,0:T(8,128)(2,1)} %wq.1, bf16[3072,1024]{1,0:T(8,128)(2,1)} %wk.1, bf16[3072,1024]{1,0:T(8,128)(2,1)} %wv.1, f32[8,128]{1,0:T(8,128)} %bitcast.1), custom_call_target="tpu_custom_call" | custom-call | flops 9663676416 | bytes 18874368 | tf_op jit(solution)/shard_map/pallas_call | solution.py:319
  44.4 2.3 %copy.7 = bf16[512,1024]{1,0:T(8,128)(2,1)} copy(bf16[512,1024]{1,0:T(8,128)(2,1)} %shard_map.55) | data formatting | bytes 2097152

commit v3 on v2

--- a/solution.py
+++ b/solution.py
@@ -11,6 +11,7 @@
 BLOCK = 512
 EPSILON = 1e-06
 MESH = pl.DeviceIdType.MESH
+SPLIT = 2
 TILE_N = 512
 TWELFTHS = (0, 4, 8, 10, 11, 12)
 CHUNKS = len(TWELFTHS) - 1
@@ -110,10 +111,10 @@
             device_id_type=MESH,
         )
 
+    for c in range(CHUNKS):
+        for j in range(1, chips):
+            y_copy(j, c, tp).start()
     sib_copy(tp).start()
-    for c in range(CHUNKS):
-        for j in range(1, chips):
-            y_copy(j, c, tp).start()
 
     own.wait()
     sib_copy(sib).wait_recv()
@@ -177,10 +178,15 @@
         else:
             wave(c, 0, 2)
 
+    part = HEAD_DIM // SPLIT
+
+    def piece(i):
+        return i // SPLIT, pl.ds(pl.multiple_of((i % SPLIT) * part, part), part)
+
     def to_partner(buffer, landing, send, recv, i):
         return pltpu.make_async_remote_copy(
-            src_ref=buffer.at[i],
-            dst_ref=landing.at[i],
+            src_ref=buffer.at[piece(i)],
+            dst_ref=landing.at[piece(i)],
             send_sem=send.at[i],
             recv_sem=recv.at[i],
             device_id={"ctx": partner, "tp": tp},
@@ -195,8 +201,8 @@
 
     def onward(i):
         return pltpu.make_async_remote_copy(
-            src_ref=pout.at[i],
-            dst_ref=pin.at[i],
+            src_ref=pout.at[piece(i)],
+            dst_ref=pin.at[piece(i)],
             send_sem=csend.at[i],
             recv_sem=crecv.at[i],
             device_id={"ctx": jnp.minimum(ctx + 2, nctx - 2 + odd), "tp": tp},
@@ -206,7 +212,8 @@
     @pl.loop(0, half)
     def _(i):
         s1[i] = whole_outer((1 - odd) * half + i).astype(BF16)
-        first(i).start()
+        for k in range(SPLIT):
+            first(SPLIT * i + k).start()
 
     @pl.loop(0, half)
     def _(i):
@@ -249,13 +256,13 @@
     def _():
         pin[...] = jnp.zeros_like(pin)
 
-    ahead = jnp.minimum(2 * pair, heads)
+    ahead = jnp.minimum(3 * pair, heads)
 
     @pl.loop(0, ahead)
     def _(h):
         intra(h)
 
-    @pl.loop(0, half)
+    @pl.loop(0, SPLIT * half)
     def _(i):
         first(i).wait_recv()
 
@@ -263,21 +270,22 @@
         def _():
             onward(i).wait_recv()
 
-        before = pin[i].astype(F32)
-        here, beside = st[odd * half + i], r1[i].astype(F32)
+        spot = piece(i)
+        before = pin[spot].astype(F32)
+        here, beside = st[odd * half + spot[0], spot[1]], r1[spot].astype(F32)
 
         @pl.when(pair < pairs - 1)
         def _():
-            pout[i] = (before + here + beside).astype(BF16)
+            pout[spot] = (before + here + beside).astype(BF16)
             onward(i).start()
 
-        s2[i] = (before + jnp.where(odd == 0, here, 0.0)).astype(BF16)
+        s2[spot] = (before + jnp.where(odd == 0, here, 0.0)).astype(BF16)
         second(i).start()
-        pown[i] = (before + jnp.where(odd == 1, beside, 0.0)).astype(BF16)
-
-        @pl.loop(jnp.minimum(ahead + 2 * i, heads), jnp.minimum(ahead + 2 * i + 2, heads))
-        def _(h):
-            intra(h)
+        pown[spot] = (before + jnp.where(odd == 1, beside, 0.0)).astype(BF16)
+
+    @pl.loop(ahead, heads)
+    def _(h):
+        intra(h)
 
     @pl.loop(0, half)
     def _(i):
@@ -285,7 +293,8 @@
 
     @pl.loop(0, half)
     def _(i):
-        second(i).wait_recv()
+        for k in range(SPLIT):
+            second(SPLIT * i + k).wait_recv()
         finish((1 - odd) * half + i, r2[i])
 
     sib_copy(tp).wait_send()
@@ -294,7 +303,7 @@
             y_copy(j, c, tp).wait_send()
             pass_on(j, c, origin(j) * 2 + core).wait_send()
 
-    @pl.loop(0, half)
+    @pl.loop(0, SPLIT * half)
     def _(i):
         first(i).wait_send()
         second(i).wait_send()
@@ -318,7 +327,7 @@
     hops = (max(chips - 1, 1), CHUNKS)
     return pl.pallas_call(
         functools.partial(kernel, nctx, ntp),
-        out_shape=jax.ShapeDtypeStruct((BLOCK, width), BF16),
+        out_shape=pltpu.VMEM((BLOCK, width), BF16),
         in_specs=[anywhere] * 4 + [vmem],
         out_specs=vmem,
         scratch_shapes=[
@@ -330,10 +339,10 @@
             pltpu.VMEM((heads, HEAD_DIM, HEAD_DIM), F32),
             small, small, small, small, small, small, small,
             dma((3 * tiles,)), dma, dma(hops), dma(hops), dma, dma, dma(hops), dma(hops),
-            dma((half,)), dma((half,)), dma((half,)), dma((half,)), dma((half,)), dma((half,)),
+            *[dma((SPLIT * half,))] * 6,
         ],
         compiler_params=pltpu.CompilerParams(
-            collective_id=0, has_side_effects=True, vmem_limit_bytes=60 * 2**20
+            collective_id=0, has_side_effects=True, vmem_limit_bytes=48 * 2**20
         ),
         cost_estimate=pl.CostEstimate(
             flops=2 * BLOCK * depth * 3 * width, bytes_accessed=6 * depth * width, transcendentals=0

time: 46.8 us -> 44.2 us (0.944)
  Pallas kernels: 44.4 us -> 41.2 us
  local copies, waits for them, and re-layouts: 2.26 us -> 2.79 us
    pallas_call x1, Pallas kernels: 44.4 us -> 41.2 us  [body(): pl.pallas_call(functools.partial(kernel, nctx, ntp), out_shape=pltpu.VMEM...]
    unnamed x1 -> x5, local copies, waits for them, and re-layouts: 2.26 us -> 2.79 us
where the time goes in v3:
time: 44.2 us; the launch traced here: 44 us
  Pallas kernels  41.2 us (93%)
  local copies, waits for them, and re-layouts  2.79 us (6%)
    pallas_call x1, Pallas kernels, body(): pl.pallas_call(functools.partial(kernel, nctx, ntp), out_shape=pltpu.VMEM...  41.2 us
    unnamed x5, local copies, waits for them, and re-layouts  2.79 us

profile of v3, /device:TPU:26, one launch (start us, length us, event | category | flops | bytes accessed | tf_op | source)
XLA Modules:
  0.0 44.0 jit_solution(9634741667841230035)
XLA Ops:
  0.0 0.0 copy-start
  0.0 1.1 %copy-done = bf16[128,3072]{1,0:T(8,128)(2,1)S(1)} copy-done((bf16[128,3072]{1,0:T(8,128)(2,1)S(1)}, bf16[128,3072]{1,0:T(8,128)(2,1)}, u32[]{:S(2)}) %copy-start) | copy-done | bytes 786456
  1.1 0.0 copy-start.1
  1.1 0.7 %copy-done.1 = f32[1024]{0:T(1024)S(1)} copy-done((f32[1024]{0:T(1024)S(1)}, f32[1024]{0:T(1024)}, u32[]{:S(2)}) %copy-start.1) | copy-done | bytes 4120
  1.8 41.2 %shard_map.55 = bf16[512,1024]{1,0:T(8,128)(2,1)S(1)} custom-call(bf16[128,3072]{1,0:T(8,128)(2,1)S(1)} %copy-done, bf16[3072,1024]{1,0:T(8,128)(2,1)} %wq.1, bf16[3072,1024]{1,0:T(8,128)(2,1)} %wk.1, bf16[3072,1024]{1,0:T(8,128)(2,1)} %wv.1, f32[8,128]{1,0:T(8,128)S(1)} %bitcast.1), custom_call_target="tpu_custom_call" | custom-call | flops 9663676416 | bytes 18874368 | tf_op jit(solution)/shard_map/pallas_call | solution.py:328
  43.0 1.0 %copy.7 = bf16[512,1024]{1,0:T(8,128)(2,1)} copy(bf16[512,1024]{1,0:T(8,128)(2,1)S(1)} %shard_map.55) | data formatting | bytes 2097152
Async XLA Ops:
  0.0 1.1 %copy-start = (bf16[128,3072]{1,0:T(8,128)(2,1)S(1)}, bf16[128,3072]{1,0:T(8,128)(2,1)}, u32[]{:S(2)}) copy-start(bf16[128,3072]{1,0:T(8,128)(2,1)} %tok.1) | copy-start | bytes 2359300
  1.1 0.7 %copy-start.1 = (f32[1024]{0:T(1024)S(1)}, f32[1024]{0:T(1024)}, u32[]{:S(2)}) copy-start(f32[1024]{0:T(1024)} %param.9) | copy-start | bytes 12292
